TPU v7x, 32 devices: a whole 2x2x4 slice. The times are simulated.
32 devices in a mesh: grp: 4 (over x, core), chan: 4 (over z), tile: 2 (over y).
Axes of the slice: x: 2, y: 2, z: 4, core: 2. Of those that a mesh axis runs over, the one named last changes fastest.
Arguments:
- voltages: bfloat16 [1024, 128, 2, 1024], P(('grp', 'tile'), 'chan'), may hold values from -6 to 6
- taps: float32 [8, 1024], replicated, may hold values from -0.0625 to 0.0625
Outputs:
- vis_real: float32 [64, 36, 128, 128], P(('grp', 'chan', 'tile'))
- vis_imag: float32 [64, 36, 128, 128], P(('grp', 'chan', 'tile'))
All inputs are finite; a program needn't handle non-finite values.
Results may differ from a plain program's by a relative error of at most 0.004.
Values may be sent and summed in bfloat16 or wider, within the bound.
A program may use at most 256 MiB of HBM per device.

v0:
```python
import functools

import jax
import jax.numpy as jnp
import numpy as np
from jax import lax
from jax.experimental import pallas as pl
from jax.experimental.pallas import tpu as pltpu
from jax.sharding import PartitionSpec as P

FRAME_SAMPLES = 1024
FILTER_TAPS = 8
CHUNK_FRAMES = 4
RIM_CHUNKS = 2
TILE_ANTENNAS = 128
LANES = 128
VMEM_LIMIT = 56 * 2**20


def transform_table(length, window):
    turns = np.arange(length)[:, None] * np.arange(window)[None, :] % length
    angles = turns * (2.0 * np.pi / length)
    return np.concatenate([np.cos(angles), np.sin(angles)], axis=1).astype(np.float32)


def regroup_matrix(window, devices):
    each = window // devices
    source = np.arange(2 * window).reshape(2, devices, each).transpose(1, 2, 0).reshape(-1)
    return np.eye(2 * window, dtype=np.float32)[source]


def filterbank_kernel(taps_ref, table_ref, volts_ref, out_ref, high, low, rows, total):
    step = pl.program_id(0)
    chunks = pl.num_programs(0) - RIM_CHUNKS
    antennas = volts_ref.shape[0]
    width = table_ref.shape[1]
    frame_rows = 2 * antennas
    chunk_rows = CHUNK_FRAMES * frame_rows

    @pl.when(step == 0)
    def _():
        total[...] = jnp.zeros_like(total)
        for tap in range(FILTER_TAPS):
            weights = taps_ref[:, tap : tap + 1] * table_ref[...]
            upper = weights.astype(jnp.bfloat16)
            columns = pl.ds(tap * width, width)
            high[:, columns] = upper
            low[:, columns] = (weights - upper.astype(jnp.float32)).astype(jnp.bfloat16)

    chunk = chunks - 1 - step

    @pl.when(chunk >= 0)
    def _():
        for frame in range(CHUNK_FRAMES):
            rows[pl.ds(frame * frame_rows, frame_rows), :] = volts_ref[:, frame].reshape(
                frame_rows, FRAME_SAMPLES
            )
        for pair in range(FILTER_TAPS // 2):
            columns = pl.ds(2 * pair * width, 2 * width)
            product = jnp.dot(
                rows[...], high[:, columns], preferred_element_type=jnp.float32
            ) + jnp.dot(rows[...], low[:, columns], preferred_element_type=jnp.float32)
            for part in range(2):
                first = (chunk * CHUNK_FRAMES + 2 * pair + part) * frame_rows
                place = pl.ds(pl.multiple_of(first, frame_rows), chunk_rows)
                for lanes in range(width // LANES):
                    begin = part * width + lanes * LANES
                    total[lanes, place, :] += product[:, begin : begin + LANES]

    half = chunk_rows // 2
    first = pl.multiple_of((chunk + RIM_CHUNKS) * chunk_rows, chunk_rows)

    def every_other(offset):
        place = pl.ds(first + offset, half, stride=2)
        return jnp.concatenate([total[i, place, :] for i in range(width // LANES)], axis=1)

    real, imaginary = every_other(0), every_other(1)
    lane = lax.broadcasted_iota(jnp.int32, (half, width), 1)
    signed = jnp.where(lane < width // 2, real, -real)
    out_ref[...] = signed + pltpu.roll(imaginary, width // 2, 1)


def filterbank(voltages, taps, table):
    antennas, frames = voltages.shape[:2]
    width = table.shape[1]
    chunks = frames // CHUNK_FRAMES
    padded = frames + RIM_CHUNKS * CHUNK_FRAMES
    return pl.pallas_call(
        filterbank_kernel,
        grid=(chunks + RIM_CHUNKS,),
        out_shape=jax.ShapeDtypeStruct((padded * antennas, width), jnp.float32),
        in_specs=[
            pl.BlockSpec((FRAME_SAMPLES, FILTER_TAPS), lambda i: (0, 0)),
            pl.BlockSpec((FRAME_SAMPLES, width), lambda i: (0, 0)),
            pl.BlockSpec(
                (antennas, CHUNK_FRAMES, 2, FRAME_SAMPLES),
                lambda i: (0, jnp.maximum(chunks - 1 - i, 0), 0, 0),
            ),
        ],
        out_specs=pl.BlockSpec(
            (CHUNK_FRAMES * antennas, width), lambda i: (chunks + RIM_CHUNKS - 1 - i, 0)
        ),
        scratch_shapes=[
            pltpu.VMEM((FRAME_SAMPLES, FILTER_TAPS * width), jnp.bfloat16),
            pltpu.VMEM((FRAME_SAMPLES, FILTER_TAPS * width), jnp.bfloat16),
            pltpu.VMEM((CHUNK_FRAMES * 2 * antennas, FRAME_SAMPLES), jnp.bfloat16),
            pltpu.VMEM((width // LANES, padded * 2 * antennas, LANES), jnp.float32),
        ],
        compiler_params=pltpu.CompilerParams(vmem_limit_bytes=VMEM_LIMIT),
    )(taps.T, table, voltages)


def regroup_kernel(order_ref, spectra_ref, rim_ref, out_ref):
    rim_rows = rim_ref.shape[0]
    rows = spectra_ref.shape[0]

    def put(first, block):
        out_ref[:, first : first + rim_rows] = lax.dot_general(
            order_ref[...],
            block.astype(jnp.bfloat16),
            (((1,), (1,)), ((), ())),
            preferred_element_type=jnp.float32,
        ).astype(jnp.bfloat16)

    put(0, spectra_ref[:rim_rows] + rim_ref[...])
    for first in range(rim_rows, rows, rim_rows):
        put(first, spectra_ref[first : first + rim_rows])


def regroup(order, spectra, rim, rows):
    width = order.shape[0]
    whole = lambda shape: pl.BlockSpec(shape, lambda i: (0, 0))
    return pl.pallas_call(
        regroup_kernel,
        grid=(1,),
        out_shape=jax.ShapeDtypeStruct((width, rows), jnp.bfloat16),
        in_specs=[whole(order.shape), whole((rows, width)), whole(rim.shape)],
        out_specs=whole((width, rows)),
        compiler_params=pltpu.CompilerParams(vmem_limit_bytes=VMEM_LIMIT),
    )(order, spectra, rim)


def correlate_kernel(scale, blocks, channel_ref, real_ref, imaginary_ref):
    depth = channel_ref.shape[1]
    matrix = channel_ref[0]
    swapped = jnp.concatenate([matrix[depth // 2 :], -matrix[: depth // 2]], axis=0)
    pair = 0
    for i in range(blocks):
        here = slice(i * TILE_ANTENNAS, (i + 1) * TILE_ANTENNAS)
        left = jnp.concatenate([matrix[:, here], swapped[:, here]], axis=1)
        product = (
            lax.dot_general(
                left,
                matrix[:, i * TILE_ANTENNAS :],
                (((0,), (0,)), ((), ())),
                preferred_element_type=jnp.float32,
            )
            * scale
        )
        for j in range(blocks - i):
            there = slice(j * TILE_ANTENNAS, (j + 1) * TILE_ANTENNAS)
            real_ref[0, pair] = product[:TILE_ANTENNAS, there]
            imaginary_ref[0, pair] = product[TILE_ANTENNAS:, there]
            pair += 1


def correlate(channel_matrix, scale):
    channels, depth, antennas = channel_matrix.shape
    blocks = antennas // TILE_ANTENNAS
    pairs = blocks * (blocks + 1) // 2
    tiles = jax.ShapeDtypeStruct((channels, pairs, TILE_ANTENNAS, TILE_ANTENNAS), jnp.float32)
    tile_spec = pl.BlockSpec((1, pairs, TILE_ANTENNAS, TILE_ANTENNAS), lambda c: (c, 0, 0, 0))
    return pl.pallas_call(
        functools.partial(correlate_kernel, scale, blocks),
        grid=(channels,),
        out_shape=(tiles, tiles),
        in_specs=[pl.BlockSpec((1, depth, antennas), lambda c: (c, 0, 0))],
        out_specs=(tile_spec, tile_spec),
        compiler_params=pltpu.CompilerParams(vmem_limit_bytes=VMEM_LIMIT),
    )(channel_matrix)


def on_device(each, voltages, taps):
    antennas, frames = voltages.shape[:2]
    groups, times, tiles = (lax.axis_size(axis) for axis in ("grp", "chan", "tile"))
    devices = groups * times * tiles
    window = each * devices
    table = jnp.asarray(transform_table(FRAME_SAMPLES, window))
    order = jnp.asarray(regroup_matrix(window, devices), jnp.bfloat16)
    spectra = filterbank(voltages, taps, table)
    rows = frames * antennas
    rim = lax.ppermute(spectra[rows:], "chan", [(i, i + 1) for i in range(times - 1)])
    leaving = regroup(order, spectra, rim, rows).reshape(devices, 2 * each, rows)
    received = lax.all_to_all(
        leaving, ("grp", "chan", "tile"), split_axis=0, concat_axis=0, tiled=True
    )
    received = received.reshape(groups, times, tiles, each, 2, frames, antennas)
    channel_matrix = received.transpose(3, 4, 1, 5, 0, 2, 6).reshape(
        each, 2 * times * frames, groups * tiles * antennas
    )
    return correlate(channel_matrix, 1.0 / (times * frames))


def solution(mesh):
    split = ("grp", "chan", "tile")
    return jax.shard_map(
        functools.partial(on_device, 2),
        mesh=mesh,
        in_specs=(P(("grp", "tile"), "chan", None, None), P()),
        out_specs=(P(split, None, None, None), P(split, None, None, None)),
        check_vma=False,
    )
```

profile of v0, /device:TPU:0, one launch (start us, length us, event | category | flops | bytes accessed | tf_op | source)
XLA Modules:
  0.0 111.7 jit_solution(8305902550849603475)
XLA Ops:
  0.6 1.8 %copy.10 = f32[8,1024]{0,1:T(8,128)} copy(f32[8,1024]{1,0:T(8,128)} %param.5) | data formatting | bytes 65536 | tf_op args[1]
  2.4 43.3 %shard_map.59.spectra_ref = f32[5120,128]{1,0:T(8,128)} custom-call(f32[1024,8]{1,0:T(8,128)} %bitcast.4, f32[1024,128]{1,0:T(8,128)} %constant.4.clone.table_ref, bf16[128,32,2,1024]{3,2,1,0:T(2,128)(2,1)} %volts_ref.1), custom_call_target="tpu_custom_call" | custom-call | tf_op jit(solution)/shard_map/pallas_call | solution.py:88
  45.7 1.1 slice.4
  46.8 5.0 %collective-permute-start = (f32[1024,128]{1,0:T(8,128)S(1)}, f32[1024,128]{1,0:T(8,128)S(1)}, u32[]{:S(2)}, u32[]{:S(2)}) collective-permute-start(f32[1024,128]{1,0:T(8,128)S(1)} %slice.4), channel_id=1, source_target_pairs={{0,2},{2,4},{4,6},{1,3},{3,5},{5,7},{8,10},{10,12},{12,14},{9,11},... | collective-permute-start | bytes 1572872 | tf_op jit(solution)/shard_map/ppermute | solution.py:192
  51.8 11.1 %collective-permute-done.rim_ref = f32[1024,128]{1,0:T(8,128)S(1)} collective-permute-done((f32[1024,128]{1,0:T(8,128)S(1)}, f32[1024,128]{1,0:T(8,128)S(1)}, u32[]{:S(2)}, u32[]{:S(2)}) %collective-permute-start) | collective-permute-done | bytes 524320 | tf_op jit(solution)/shard_map/ppermute | solution.py:192
  62.9 0.0 copy-start
  62.9 0.8 copy-done
  63.7 3.1 %shard_map.60 = bf16[128,4096]{1,0:T(8,128)(2,1)} custom-call(bf16[128,128]{1,0:T(8,128)(2,1)} %constant.5.clone.order_ref, f32[5120,128]{1,0:T(8,128)} %shard_map.59.spectra_ref, f32[1024,128]{1,0:T(8,128)} %copy-done), custom_call_target="tpu_custom_call" | custom-call | tf_op jit(solution)/shard_map/pallas_call | solution.py:133
  66.8 1.5 %reshape.13 = bf16[32,4,4096]{2,1,0:T(4,128)(2,1)S(1)} reshape(bf16[128,4096]{1,0:T(8,128)(2,1)} %shard_map.60) | data formatting | bytes 2097152 | tf_op jit(solution)/shard_map/reshape | solution.py:193
  68.2 34.1 %all_to_all.5 = bf16[32,4,4096]{2,1,0:T(4,128)(2,1)S(1)} all-to-all(bf16[32,4,4096]{2,1,0:T(4,128)(2,1)S(1)} %reshape.13), channel_id=1, replica_groups=mesh['grp'=4,'chan'=4,'tile'=2] {'grp','chan','tile'}, dimensions={0} | all-to-all | bytes 2097152 | tf_op jit(solution)/shard_map/all_to_all | solution.py:194
  102.4 1.1 reshape.16
  103.5 1.1 copy.12
  104.6 1.5 %reshape.15.channel_ref = bf16[2,256,1024]{2,1,0:T(8,128)(2,1)} reshape(bf16[2,2,4,32,4,2,128]{6,5,4,3,2,1,0:T(2,128)(2,1)S(1)} %copy.12) | data formatting | bytes 2097152 | tf_op jit(solution)/shard_map/reshape | solution.py:198
  106.1 5.6 %shard_map.61 = (f32[2,36,128,128]{3,2,1,0:T(8,128)}, f32[2,36,128,128]{3,2,1,0:T(8,128)}) custom-call(bf16[2,256,1024]{2,1,0:T(8,128)(2,1)} %reshape.15.channel_ref), custom_call_target="tpu_custom_call" | custom-call | tf_op jit(solution)/shard_map/pallas_call | solution.py:173
Async XLA Ops:
  46.8 16.1 %collective-permute-start = (f32[1024,128]{1,0:T(8,128)S(1)}, f32[1024,128]{1,0:T(8,128)S(1)}, u32[]{:S(2)}, u32[]{:S(2)}) collective-permute-start(f32[1024,128]{1,0:T(8,128)S(1)} %slice.4), channel_id=1, source_target_pairs={{0,2},{2,4},{4,6},{1,3},{3,5},{5,7},{8,10},{10,12},{12,14},{9,11},... | collective-permute-start | bytes 1572872 | tf_op jit(solution)/shard_map/ppermute | solution.py:192
  62.9 0.8 copy-start
where the time goes:
time: 112 us
  Pallas kernels  52 us (46%)
  blocking collectives  34.1 us (30%)
  waiting for transfers between devices  11.1 us (10%)
  local copies, waits for them, and re-layouts  8.79 us (8%)
  starting transfers between devices  4.96 us (4%)
    pallas_call x1, Pallas kernels, filterbank(): pl.pallas_call(filterbank_kernel, grid=(chunks + RIM_CHUNKS,), out_shape=...  43.3 us
    all_to_all x1, blocking collectives, on_device(): lax.all_to_all(leaving, ('grp', 'chan', 'tile'), split_axis=0, concat_axi...  34.1 us
    ppermute x1, waiting for transfers between devices, on_device(): lax.ppermute(spectra[rows:], 'chan', [(i, i + 1) for i in range(times - 1)])  11.1 us
    pallas_call x1, Pallas kernels, correlate(): pl.pallas_call(functools.partial(correlate_kernel, scale, blocks), grid=(...  5.55 us
    ppermute x1, starting transfers between devices, on_device(): lax.ppermute(spectra[rows:], 'chan', [(i, i + 1) for i in range(times - 1)])  4.96 us
    pallas_call x1, Pallas kernels, regroup(): pl.pallas_call(regroup_kernel, grid=(1,), out_shape=jax.ShapeDtypeStruct(...  3.1 us
    unnamed x3, local copies, waits for them, and re-layouts  2.53 us
  transfers between devices with their start and end apart: 1, of which 1 were waited for; matrix products, arithmetic and copies ran while one was open for 0% of the time, Pallas kernels for 0%

commit v1 on v0

v1 whole, which is shorter than its diff:
```python
import functools
import math

import jax
import jax.numpy as jnp
import numpy as np
from jax import lax
from jax.experimental import pallas as pl
from jax.experimental.pallas import tpu as pltpu
from jax.sharding import PartitionSpec as P

FRAME_SAMPLES = 1024
FILTER_TAPS = 8
CHUNK_FRAMES = 4
RIM_CHUNKS = 2
SEND_ROWS = 16
TURN_ROWS = 256
TILE_ANTENNAS = 128
LANES = 128
VMEM_LIMIT = 58 * 2**20


def transform_table(length, window):
    turns = np.arange(length)[:, None] * np.arange(window)[None, :] % length
    angles = turns * (2.0 * np.pi / length)
    return np.concatenate([np.cos(angles), np.sin(angles)], axis=1).astype(np.float32)


def turn_matrix():
    matrix = np.zeros((TURN_ROWS, TURN_ROWS), np.float32)
    even = np.arange(0, TURN_ROWS, 2)
    matrix[even, even + 1] = 1.0
    matrix[even + 1, even] = -1.0
    return matrix


def spectra_kernel(
    sizes,
    taps_ref,
    table_ref,
    volts_ref,
    channel_ref,
    high,
    low,
    rows,
    total,
    spectra,
    turned,
    leaving,
    rim_out,
    rim_in,
    send_sem,
    recv_sem,
    own_sem,
    rim_send_sem,
    rim_recv_sem,
):
    groups, times, tiles, frames = sizes
    devices = groups * times * tiles
    step = pl.program_id(0)
    chunks = frames // CHUNK_FRAMES
    antennas = volts_ref.shape[0]
    width = table_ref.shape[1]
    window = width // 2
    frame_rows = 2 * antennas
    chunk_rows = CHUNK_FRAMES * frame_rows
    half = chunk_rows // 2
    group, time, tile = (lax.axis_index(axis) for axis in ("grp", "chan", "tile"))
    me = (group * times + time) * tiles + tile

    def place_of(device):
        return (
            lax.div(device, times * tiles),
            lax.rem(lax.div(device, tiles), times),
            lax.rem(device, tiles),
        )

    @pl.when(step == 0)
    def _():
        barrier = pltpu.get_barrier_semaphore()

        @pl.loop(1, devices)
        def _(distance):
            pl.semaphore_signal(
                barrier,
                inc=1,
                device_id=place_of(lax.rem(me + distance, devices)),
                device_id_type=pl.DeviceIdType.MESH,
            )

        total[...] = jnp.zeros_like(total)
        taps = taps_ref[...].T
        for tap in range(FILTER_TAPS):
            weights = taps[:, tap : tap + 1] * table_ref[...]
            upper = weights.astype(jnp.bfloat16)
            columns = pl.ds(tap * width, width)
            high[:, columns] = upper
            low[:, columns] = (weights - upper.astype(jnp.float32)).astype(jnp.bfloat16)

    chunk = chunks - 1 - step

    @pl.when(chunk >= 0)
    def _():
        for frame in range(CHUNK_FRAMES):
            rows[pl.ds(frame * frame_rows, frame_rows), :] = volts_ref[:, frame].reshape(
                frame_rows, FRAME_SAMPLES
            )
        for pair in range(FILTER_TAPS // 2):
            columns = pl.ds(2 * pair * width, 2 * width)
            product = jnp.dot(
                rows[...], high[:, columns], preferred_element_type=jnp.float32
            ) + jnp.dot(rows[...], low[:, columns], preferred_element_type=jnp.float32)
            for part in range(2):
                first = (chunk * CHUNK_FRAMES + 2 * pair + part) * frame_rows
                place = pl.ds(pl.multiple_of(first, frame_rows), chunk_rows)
                for lanes in range(width // LANES):
                    begin = part * width + lanes * LANES
                    total[lanes, place, :] += product[:, begin : begin + LANES]

    done = chunk + RIM_CHUNKS
    first = pl.multiple_of(done * chunk_rows, chunk_rows)

    def every_other(offset):
        place = pl.ds(first + offset, half, stride=2)
        return jnp.concatenate([total[i, place, :] for i in range(width // LANES)], axis=1)

    real, imaginary = every_other(0), every_other(1)
    lane = lax.broadcasted_iota(jnp.int32, (half, width), 1)
    signed = jnp.where(lane < window, real, -real)
    spectra[...] = signed + pltpu.roll(imaginary, window, 1)

    def rim_copy(slot):
        return pltpu.make_async_remote_copy(
            src_ref=rim_out.at[slot],
            dst_ref=rim_in.at[slot],
            send_sem=rim_send_sem.at[slot],
            recv_sem=rim_recv_sem.at[slot],
            device_id=(group, lax.rem(time + 1, times), tile),
            device_id_type=pl.DeviceIdType.MESH,
        )

    @pl.when(step == 0)
    def _():
        pl.semaphore_wait(pltpu.get_barrier_semaphore(), devices - 1)

    for slot in range(RIM_CHUNKS):

        @pl.when(done == chunks + slot)
        def _():
            rim_out[slot] = spectra[...]

            @pl.when(time < times - 1)
            def _():
                rim_copy(slot).start()

        @pl.when((done == slot) & (time > 0))
        def _():
            rim_copy(slot).wait_recv()
            spectra[...] += rim_in[slot]

    @pl.when(done < chunks)
    def _():
        late = lax.rem(done, 2)
        for frame in range(CHUNK_FRAMES):
            block = spectra[pl.ds(frame * antennas, antennas), :].T
            for part in range(2):
                row = (late * CHUNK_FRAMES + frame) * 2 + part
                turned[pl.ds(row, window, stride=SEND_ROWS), :] = block[
                    part * window : (part + 1) * window
                ]

    @pl.when((done < chunks) & (lax.rem(done, 2) == 0))
    def _():
        send = lax.div(done, 2)
        leaving[send] = turned[...].astype(jnp.bfloat16).reshape(leaving.shape[1:])
        top = pl.multiple_of(time * (2 * frames) + send * SEND_ROWS, SEND_ROWS)
        left = pl.multiple_of((group * tiles + tile) * antennas, antennas)
        landing = channel_ref.at[:, pl.ds(top, SEND_ROWS), pl.ds(left, antennas)]

        @pl.loop(1, devices)
        def _(distance):
            device = lax.rem(me + distance, devices)
            pltpu.make_async_remote_copy(
                src_ref=leaving.at[send, device],
                dst_ref=landing,
                send_sem=send_sem,
                recv_sem=recv_sem,
                device_id=place_of(device),
                device_id_type=pl.DeviceIdType.MESH,
            ).start()

        pltpu.make_async_copy(leaving.at[send, me], landing, own_sem.at[send]).start()

    @pl.when(done == 0)
    def _():
        for send in range(chunks // 2):
            top = pl.multiple_of(time * (2 * frames) + send * SEND_ROWS, SEND_ROWS)
            left = pl.multiple_of((group * tiles + tile) * antennas, antennas)
            landing = channel_ref.at[:, pl.ds(top, SEND_ROWS), pl.ds(left, antennas)]
            pltpu.make_async_copy(leaving.at[send, me], landing, own_sem.at[send]).wait()

        @pl.when(time < times - 1)
        def _():
            for slot in range(RIM_CHUNKS):
                rim_copy(slot).wait_send()

        others = leaving.at[:, pl.ds(0, devices - 1)]
        pltpu.make_async_copy(others, others, send_sem).wait()
        pltpu.make_async_copy(others, others, recv_sem).wait()


def spectra_by_channel(sizes, each, voltages, taps, table):
    groups, times, tiles = sizes
    devices = groups * times * tiles
    antennas, frames = voltages.shape[:2]
    width = table.shape[1]
    chunks = frames // CHUNK_FRAMES
    padded = frames + RIM_CHUNKS * CHUNK_FRAMES
    rim = (RIM_CHUNKS, CHUNK_FRAMES * antennas, width)
    weights = (FRAME_SAMPLES, FILTER_TAPS * width)
    return pl.pallas_call(
        functools.partial(spectra_kernel, (*sizes, frames)),
        grid=(chunks + RIM_CHUNKS,),
        out_shape=jax.ShapeDtypeStruct(
            (each, 2 * times * frames, groups * tiles * antennas), jnp.bfloat16
        ),
        in_specs=[
            pl.BlockSpec((FILTER_TAPS, FRAME_SAMPLES), lambda i: (0, 0)),
            pl.BlockSpec(
                (FRAME_SAMPLES, width), lambda i: (0, 0), pipeline_mode=pl.Buffered(1)
            ),
            pl.BlockSpec(
                (antennas, CHUNK_FRAMES, 2, FRAME_SAMPLES),
                lambda i: (0, jnp.maximum(chunks - 1 - i, 0), 0, 0),
            ),
        ],
        out_specs=pl.BlockSpec(memory_space=pl.ANY),
        scratch_shapes=[
            pltpu.VMEM(weights, jnp.bfloat16),
            pltpu.VMEM(weights, jnp.bfloat16),
            pltpu.VMEM((CHUNK_FRAMES * 2 * antennas, FRAME_SAMPLES), jnp.bfloat16),
            pltpu.VMEM((width // LANES, padded * 2 * antennas, LANES), jnp.float32),
            pltpu.VMEM(rim[1:], jnp.float32),
            pltpu.VMEM((width // 2 * SEND_ROWS, antennas), jnp.float32),
            pltpu.VMEM((chunks // 2, devices, each, SEND_ROWS, antennas), jnp.bfloat16),
            pltpu.VMEM(rim, jnp.float32),
            pltpu.VMEM(rim, jnp.float32),
            pltpu.SemaphoreType.DMA,
            pltpu.SemaphoreType.DMA,
            pltpu.SemaphoreType.DMA((chunks // 2,)),
            pltpu.SemaphoreType.DMA((RIM_CHUNKS,)),
            pltpu.SemaphoreType.DMA((RIM_CHUNKS,)),
        ],
        compiler_params=pltpu.CompilerParams(
            vmem_limit_bytes=VMEM_LIMIT, collective_id=0, has_side_effects=True
        ),
    )(taps, table, voltages)


def correlate_kernel(scale, blocks, turn_ref, channel_ref, real_ref, imaginary_ref):
    depth = channel_ref.shape[1]
    matrix = channel_ref[0]
    swapped = jnp.concatenate(
        [
            jnp.dot(
                turn_ref[...],
                matrix[top : top + TURN_ROWS],
                preferred_element_type=jnp.float32,
            ).astype(jnp.bfloat16)
            for top in range(0, depth, TURN_ROWS)
        ],
        axis=0,
    )
    pair = 0
    for i in range(blocks):
        here = slice(i * TILE_ANTENNAS, (i + 1) * TILE_ANTENNAS)
        left = jnp.concatenate([matrix[:, here], swapped[:, here]], axis=1)
        product = (
            lax.dot_general(
                left,
                matrix[:, i * TILE_ANTENNAS :],
                (((0,), (0,)), ((), ())),
                preferred_element_type=jnp.float32,
            )
            * scale
        )
        for j in range(blocks - i):
            there = slice(j * TILE_ANTENNAS, (j + 1) * TILE_ANTENNAS)
            real_ref[0, pair] = product[:TILE_ANTENNAS, there]
            imaginary_ref[0, pair] = product[TILE_ANTENNAS:, there]
            pair += 1


def correlate(channel_matrix, scale):
    channels, depth, antennas = channel_matrix.shape
    blocks = antennas // TILE_ANTENNAS
    pairs = blocks * (blocks + 1) // 2
    tiles = jax.ShapeDtypeStruct((channels, pairs, TILE_ANTENNAS, TILE_ANTENNAS), jnp.float32)
    tile_spec = pl.BlockSpec((1, pairs, TILE_ANTENNAS, TILE_ANTENNAS), lambda c: (c, 0, 0, 0))
    return pl.pallas_call(
        functools.partial(correlate_kernel, scale, blocks),
        grid=(channels,),
        out_shape=(tiles, tiles),
        in_specs=[
            pl.BlockSpec((TURN_ROWS, TURN_ROWS), lambda c: (0, 0)),
            pl.BlockSpec((1, depth, antennas), lambda c: (c, 0, 0)),
        ],
        out_specs=(tile_spec, tile_spec),
        compiler_params=pltpu.CompilerParams(vmem_limit_bytes=VMEM_LIMIT),
    )(jnp.asarray(turn_matrix(), jnp.bfloat16), channel_matrix)


def on_device(each, voltages, taps):
    sizes = tuple(lax.axis_size(axis) for axis in ("grp", "chan", "tile"))
    table = jnp.asarray(transform_table(FRAME_SAMPLES, each * math.prod(sizes)))
    channel_matrix = spectra_by_channel(sizes, each, voltages, taps, table)
    return correlate(channel_matrix, 1.0 / (sizes[1] * voltages.shape[1]))


def solution(mesh):
    split = ("grp", "chan", "tile")
    return jax.shard_map(
        functools.partial(on_device, 2),
        mesh=mesh,
        in_specs=(P(("grp", "tile"), "chan", None, None), P()),
        out_specs=(P(split, None, None, None), P(split, None, None, None)),
        check_vma=False,
    )
```

time: 112 us -> 68.5 us (0.61)
  blocking collectives: 34.1 us -> 0 us
  Pallas kernels: 52 us -> 67.7 us
  waiting for transfers between devices: 11.1 us -> 0 us
  local copies, waits for them, and re-layouts: 8.79 us -> 0 us
  starting transfers between devices: 4.96 us -> 0 us
    all_to_all x1 -> x0, blocking collectives: 34.1 us -> none  [on_device(): lax.all_to_all(leaving, ('grp', 'chan', 'tile'), split_axis=0, concat_axi...]
    pallas_call x2 -> x1, Pallas kernels: 46.4 us -> 61.9 us  [spectra_by_channel(): pl.pallas_call(functools.partial(spectra_kernel, (*sizes, frames)), grid=...]
    ppermute x1 -> x0, waiting for transfers between devices: 11.1 us -> none  [on_device(): lax.ppermute(spectra[rows:], 'chan', [(i, i + 1) for i in range(times - 1)])]
    ppermute x1 -> x0, starting transfers between devices: 4.96 us -> none  [on_device(): lax.ppermute(spectra[rows:], 'chan', [(i, i + 1) for i in range(times - 1)])]
    reshape x3 -> x0, local copies, waits for them, and re-layouts: 4.1 us -> none  [the longest x1 1.54 us: on_device(): received.transpose(3, 4, 1, 5, 0, 2, 6)]
    unnamed x3 -> x0, local copies, waits for them, and re-layouts: 2.53 us -> none
  transfers between devices with their start and end apart: 1 -> 0, of which waited for: 1 -> 0; matrix products, arithmetic and copies ran while one was open for 0% -> 0% of each run, Pallas kernels for 0% -> 0%
where the time goes in v1:
time: 68.5 us; the launch traced here: 68.3 us
  Pallas kernels  67.7 us (99%)
    pallas_call x1, Pallas kernels, spectra_by_channel(): pl.pallas_call(functools.partial(spectra_kernel, (*sizes, frames)), grid=...  61.9 us
    pallas_call x1, Pallas kernels, correlate(): pl.pallas_call(functools.partial(correlate_kernel, scale, blocks), grid=(...  5.78 us

profile of v1, /device:TPU:0, one launch (start us, length us, event | category | flops | bytes accessed | tf_op | source)
XLA Modules:
  0.0 68.3 jit_solution(15517400180652908503)
XLA Ops:
  0.6 61.9 %shard_map.59.channel_ref = bf16[2,256,1024]{2,1,0:T(8,128)(2,1)} custom-call(f32[8,1024]{1,0:T(8,128)} %taps_ref.1, f32[1024,128]{1,0:T(8,128)} %constant.4.clone.table_ref, bf16[128,32,2,1024]{3,2,1,0:T(2,128)(2,1)} %volts_ref.1), custom_call_target="tpu_custom_call" | custom-call | tf_op jit(solution)/shard_map/pallas_call | solution.py:221
  62.6 5.8 %shard_map.60 = (f32[2,36,128,128]{3,2,1,0:T(8,128)}, f32[2,36,128,128]{3,2,1,0:T(8,128)}) custom-call(bf16[256,256]{1,0:T(8,128)(2,1)} %constant.5.clone.turn_ref, bf16[2,256,1024]{2,1,0:T(8,128)(2,1)} %shard_map.59.channel_ref), custom_call_target="tpu_custom_call" | custom-call | tf_op jit(solution)/shard_map/pallas_call | solution.py:300
